TPU v7x, 512 devices: a whole 4x4x16 slice. The times are simulated.
512 devices in a mesh: dp: 32 (over z_lo, y), pipe: 16 (over z_hi, x, core).
Axes of the slice: x: 4, y: 4, z: 16 (z_hi: 2, z_lo: 8; z = z_hi * 8 + z_lo), core: 2. Of those that a mesh axis runs over, the one named last changes fastest.
Arguments:
- tokens: bfloat16 [65536, 4096], P(('dp', 'pipe')), may hold values from -24 to 24
- cotangent: bfloat16 [65536, 4096], P(('dp', 'pipe')), may hold values from -6 to 6
- gate_weight: bfloat16 [256, 4096], P('pipe'), may hold values from -0.09375 to 0.09375
- up_weight: bfloat16 [256, 4096], P('pipe'), may hold values from -0.09375 to 0.09375
- down_weight: bfloat16 [256, 4096], P('pipe'), may hold values from -0.375 to 0.375
Outputs:
- input_grad: bfloat16 [65536, 4096], P(('dp', 'pipe'))
- gate_grad: float32 [256, 4096], P('pipe', 'dp')
- up_grad: float32 [256, 4096], P('pipe', 'dp')
- down_grad: float32 [256, 4096], P('pipe', 'dp')
All inputs are finite; a program needn't handle non-finite values.
Results may differ from a plain program's by a relative error of at most 0.005.
Values may be sent and summed in bfloat16 or wider, within the bound.
A program may use at most 64 MiB of HBM per device.

v0:
```python
import jax
import jax.numpy as jnp
from jax import lax
from jax.sharding import PartitionSpec as P


def per_device(tokens, cotangent, gate_weight, up_weight, down_weight):
    tok_count, feature_count = tokens.shape
    slab_rows = gate_weight.shape[0]
    sections = lax.axis_size("pipe")
    token_total = tok_count * lax.axis_size("dp") * sections
    grad_scale = float(token_total) ** (-0.5)
    contract_feat = (((1,), (1,)), ((), ()))
    contract_tok = (((0,), (0,)), ((), ()))
    gate_rows = lax.all_gather(gate_weight, "pipe", axis=0, tiled=True)
    up_rows = lax.all_gather(up_weight, "pipe", axis=0, tiled=True)
    down_rows = lax.all_gather(down_weight, "pipe", axis=0, tiled=True)
    gate_val = lax.dot_general(tokens, gate_rows, contract_feat, preferred_element_type=jnp.float32)
    up_val = lax.dot_general(tokens, up_rows, contract_feat, preferred_element_type=jnp.float32)
    sigma = jax.nn.sigmoid(gate_val)
    silu_val = gate_val * sigma
    hidden = (silu_val * up_val).astype(jnp.bfloat16)
    back = lax.dot_general(cotangent, down_rows, contract_feat, preferred_element_type=jnp.float32)
    up_back = (back * silu_val).astype(jnp.bfloat16)
    gate_back = (back * up_val * sigma * (1.0 + gate_val * (1.0 - sigma))).astype(jnp.bfloat16)
    in_sum = jnp.dot(gate_back, gate_rows, preferred_element_type=jnp.float32)
    in_sum = in_sum + jnp.dot(up_back, up_rows, preferred_element_type=jnp.float32)
    gate_term = lax.dot_general(gate_back, tokens, contract_tok, preferred_element_type=jnp.float32)
    up_term = lax.dot_general(up_back, tokens, contract_tok, preferred_element_type=jnp.float32)
    down_term = lax.dot_general(hidden, cotangent, contract_tok, preferred_element_type=jnp.float32)
    fresh = jnp.stack([gate_term, up_term, down_term]).astype(jnp.bfloat16)
    terms = fresh
    in_sum, terms = (in_sum, terms)
    grouped = terms.reshape(3, sections, slab_rows, feature_count)
    received = lax.all_to_all(grouped, "pipe", split_axis=1, concat_axis=1, tiled=True)
    summed = jnp.sum(received.astype(jnp.float32), axis=1)
    shares = lax.psum_scatter(summed, "dp", scatter_dimension=2, tiled=True)
    shares = shares * grad_scale
    return (in_sum.astype(jnp.bfloat16), shares[0], shares[1], shares[2])


def solution(mesh):
    in_specs = (
        P(("dp", "pipe"), None),
        P(("dp", "pipe"), None),
        P("pipe", None),
        P("pipe", None),
        P("pipe", None),
    )
    out_specs = (P(("dp", "pipe"), None), P("pipe", "dp"), P("pipe", "dp"), P("pipe", "dp"))
    return jax.shard_map(
        per_device, mesh=mesh, in_specs=in_specs, out_specs=out_specs, check_vma=False
    )
```

profile of v0, /device:TPU:2, one launch (start us, length us, event | category | flops | bytes accessed | tf_op | source)
XLA Modules:
  0.0 816.3 jit_solution(4946939356332541235)
XLA Ops:
  7.2 0.0 copy-start
  7.2 0.0 all-gather.6.cloned.1.call-start
  7.2 0.7 all-gather.6.cloned.1.call-update
  7.9 0.0 all-gather.8.cloned.1.call-start
  8.0 0.7 all-gather.8.cloned.1.call-update
  8.7 0.0 all-gather.4.cloned.1.call-start
  8.7 0.7 all-gather.4.cloned.1.call-update
  9.4 0.0 reduce-scatter.2.cloned.1.call-start
  9.4 98.2 %all-gather.6.cloned.1.call-done = bf16[256,4096]{1,0:T(8,128)(2,1)} async-done(((bf16[16,4096]{1,0:T(8,128)(2,1)}), bf16[256,4096]{1,0:T(8,128)(2,1)}) %all-gather.6.cloned.1.call-update) | async-done | bytes 2097168 | tf_op jit(solution)/shard_map/all_gather | solution.py:16
  107.6 0.0 copy-done
  107.6 2.4 fusion.4
  110.1 83.8 %all-gather.8.cloned.1.call-done = bf16[256,4096]{1,0:T(8,128)(2,1)} async-done(((bf16[16,4096]{1,0:T(8,128)(2,1)}), bf16[256,4096]{1,0:T(8,128)(2,1)}) %all-gather.8.cloned.1.call-update) | async-done | bytes 2097168 | tf_op jit(solution)/shard_map/all_gather | solution.py:15
  193.9 0.0 copy-start.3
  193.9 2.5 fusion.5
  196.4 0.0 copy-done.3
  196.4 0.8 convolution_convert_fusion
  197.2 83.0 %all-gather.4.cloned.1.call-done = bf16[256,4096]{1,0:T(8,128)(2,1)} async-done(((bf16[16,4096]{1,0:T(8,128)(2,1)}), bf16[256,4096]{1,0:T(8,128)(2,1)}) %all-gather.4.cloned.1.call-update) | async-done | bytes 2097168 | tf_op jit(solution)/shard_map/all_gather | solution.py:17
  280.2 2.8 multiply_convert_fusion.1
  283.0 0.7 convolution_convert_fusion.1
  283.7 0.7 convolution_convert_fusion.2
  284.4 1.0 pad_maximum_fusion
  285.4 134.1 %all_to_all.5 = bf16[3,16,16,4096]{3,2,0,1:T(8,128)(2,1)S(1)} all-to-all(bf16[3,16,16,4096]{3,2,0,1:T(8,128)(2,1)S(1)} %pad_maximum_fusion), channel_id=1, replica_groups=mesh['dp'=32,'pipe'=16] {'pipe'}, dimensions={1} | all-to-all | bytes 12582912 | tf_op jit(solution)/shard_map/all_to_all | solution.py:35
  419.6 2.1 convert_reduce_fusion
  421.7 0.0 reduce-scatter.2.cloned.1.call-update
  421.7 0.0 copy-done.1
  421.7 0.0 copy-start.2
  421.7 0.5 fusion.6
  422.2 1.1 copy-done.2
  423.3 1.4 fusion
  424.7 383.6 %reduce-scatter.2.cloned.1.call-done = f32[3,16,128]{2,1,0:T(8,128)} async-done(((f32[3,16,4096]{2,1,0:T(8,128)}), f32[3,16,128]{2,1,0:T(8,128)}) %reduce-scatter.2.cloned.1.call-update) | async-done | bytes 24592 | tf_op jit(solution)/shard_map/reduce_scatter | solution.py:37
  808.4 0.7 broadcast_multiply_fusion
  809.1 0.6 slice_bitcast_fusion
  (1 shorter events, 0.0 us)
Async XLA Ops:
  7.2 100.5 %copy-start = (bf16[128,4096]{1,0:T(8,128)(2,1)S(1)}, bf16[128,4096]{1,0:T(8,128)(2,1)}, u32[]{:S(2)}) copy-start(bf16[128,4096]{1,0:T(8,128)(2,1)} %param.5) | copy-start | bytes 3145732
  7.2 100.5 %all-gather.6.cloned.1.call-start = ((), (), s32[]{:S(2)}) async-start(), calls=%async_computation.3 | async-start | bytes 2228224 | tf_op jit(solution)/shard_map/all_gather | solution.py:16
  7.9 186.0 %all-gather.8.cloned.1.call-start = ((), (), s32[]{:S(2)}) async-start(), calls=%async_computation.4 | async-start | bytes 2228224 | tf_op jit(solution)/shard_map/all_gather | solution.py:15
  8.7 271.5 %all-gather.4.cloned.1.call-start = ((), (), s32[]{:S(2)}) async-start(), calls=%async_computation.2 | async-start | bytes 2228224 | tf_op jit(solution)/shard_map/all_gather | solution.py:17
  9.4 799.0 %reduce-scatter.2.cloned.1.call-start = ((), (), s32[]{:S(2)}) async-start(), calls=%async_computation.5 | async-start | bytes 811008 | tf_op jit(solution)/shard_map/reduce_scatter | solution.py:37
  193.9 2.5 copy-start.3
  419.6 2.1 copy-start.1
  421.7 1.6 copy-start.2
Sparse Core Ops, SparseCore 0:
  11.3 96.2 all-gather.5
  111.0 82.9 all-gather.7
  197.2 82.9 all-gather.3
  421.8 386.5 reduce-scatter.1
where the time goes:
time: 817 us; the launch traced here: 816 us
  waiting for transfers between devices  651 us (80%)
  blocking collectives  134 us (16%)
  between operations  13.9 us (2%)
  matrix products  11.8 us (1%)
    reduce_scatter x1, waiting for transfers between devices, per_device(): shares = lax.psum_scatter(summed, 'dp', scatter_dimension=2, tiled=True)  384 us
    all_to_all x1, blocking collectives, per_device(): lax.all_to_all(grouped, 'pipe', split_axis=1, concat_axis=1, tiled=True)  134 us
    all_gather x1, waiting for transfers between devices, per_device(): up_rows = lax.all_gather(up_weight, 'pipe', axis=0, tiled=True)  98.2 us
    all_gather x1, waiting for transfers between devices, per_device(): gate_rows = lax.all_gather(gate_weight, 'pipe', axis=0, tiled=True)  83.8 us
    all_gather x1, waiting for transfers between devices, per_device(): down_rows = lax.all_gather(down_weight, 'pipe', axis=0, tiled=True)  83 us
  transfers between devices with their start and end apart: 4, of which 4 were waited for; matrix products, arithmetic and copies ran while one was open for 1% of the time, Pallas kernels for 0%

commit v1 on v0

v1 whole, which is shorter than its diff:
```python
import jax
import jax.numpy as jnp
from jax import lax
from jax.experimental import pallas as pl
from jax.experimental.pallas import tpu as pltpu
from jax.sharding import PartitionSpec as P

F32, BF16 = jnp.float32, jnp.bfloat16
MESH = pl.DeviceIdType.MESH
NX, NY, ZLO, NZ = 4, 4, 8, 16
GATE, UP, DOWN = 0, 1, 2


def panel_kernel(
    scale,
    tok_in, cot_in, wg_in, wu_in, wd_in,
    ig_out, gg_out, ug_out, dg_out,
    tok, cot, w, act, ta, tb, ra, rb, ua, ub, va, vb, zs, zr, ig_send, ig_recv, ig_own,
    load_sem, core_s, core_r, own_xs, own_xr, own_ys, own_yr, hz_s, hz_r, o1_s, o1_r, o2_s, o2_r,
    p1_s, p1_r, p2_s, p2_r, z_s, z_r,
):
    dp, pipe = lax.axis_index("dp"), lax.axis_index("pipe")
    zl, y = dp // NY, dp % NY
    zh, x, c = pipe // 8, (pipe // 2) % NX, pipe % 2
    z = zh * ZLO + zl

    def dev(x_, y_, z_, c_):
        return ((z_ % ZLO) * NY + y_, ((z_ // ZLO) * NX + x_) * 2 + c_)

    def xdev(d):
        return dev((x + d) % NX, y, z, c)

    def ydev(d):
        return dev(x, (y + d) % NY, z, c)

    def zdev(z_):
        return dev(x, y, z_ % NZ, c)

    partner = dev(x, y, z, 1 - c)

    def push(src, dst, ssem, rsem, to):
        pltpu.make_async_remote_copy(src, dst, ssem, rsem, device_id=to, device_id_type=MESH).start()

    def drain(ref, sem):
        pltpu.make_async_copy(ref, ref, sem).wait()

    loads = [
        pltpu.make_async_copy(src, dst, load_sem.at[i])
        for i, (src, dst) in enumerate([
            (wg_in, w.at[GATE, 0:16]), (wu_in, w.at[UP, 0:16]), (wd_in, w.at[DOWN, 0:16]),
            (tok_in, tok.at[0:128]), (cot_in, cot.at[0:128]),
        ])
    ]
    for cp in loads:
        cp.start()

    barrier = pltpu.get_barrier_semaphore()

    def greet(to):
        pl.semaphore_signal(barrier, inc=1, device_id=to, device_id_type=MESH)

    greet(partner)
    for d in range(1, 4):
        greet(xdev(d))
        greet(ydev(d))

    @pl.loop(1, NZ)
    def _(d):
        greet(zdev(z + d))

    pl.semaphore_wait(barrier, 7 + NZ - 1)

    quarter = pl.ds(pl.multiple_of(y * 1024, 1024), 1024)
    eighth0 = pl.ds(pl.multiple_of(y * 512, 512), 512)
    eighth1 = pl.ds(pl.multiple_of(2048 + y * 512, 512), 512)
    pieces = [(GATE, quarter, 1024), (UP, eighth0, 512), (UP, eighth1, 512), (DOWN, quarter, 1024)]

    def from_x(d):
        return pl.ds(16 * (4 - d), 16)

    def other_from_x(d):
        return pl.ds(64 + 16 * (4 - d), 16)

    for cp in loads[:3]:
        cp.wait()
    for t in (GATE, UP):
        for d in (2, 1, 3):
            push(w.at[t, 0:16, quarter], w.at[t, from_x(d), quarter], own_xs.at[t], own_xr.at[t], xdev(d))
    at_edge = (zl == 0) | (zl == ZLO - 1)
    step = jnp.where(zl == 0, NZ - 1, 1)

    @pl.when(at_edge)
    def _():
        for p, (t, cols, _) in enumerate(pieces):
            for dist in (4, 3, 2, 1):
                push(w.at[t, 0:16, cols], w.at[t, 64:80, cols], hz_s.at[p], hz_r.at[p], zdev(z + step * dist))

    for d in (2, 1, 3):
        push(w.at[DOWN, 0:16], w.at[DOWN, from_x(d)], own_xs.at[DOWN], own_xr.at[DOWN], xdev(d))
    loads[3].wait()
    push(tok.at[0:128], tok.at[128:256], core_s.at[0], core_r.at[0], partner)
    loads[4].wait()
    push(cot.at[0:128], cot.at[128:256], core_s.at[1], core_r.at[1], partner)

    for t in (GATE, UP):
        drain(w.at[t, 0:48, 0:1024], own_xr.at[t])
        for d in (2, 1, 3):
            push(w.at[t, 16:64, quarter], w.at[t, 16:64, quarter], own_ys.at[t], own_yr.at[t], ydev(d))

    for p, (t, cols, n) in enumerate(pieces):
        drain(w.at[t, 0:16, 0:n], hz_r.at[p])
        for d in (2, 1, 3):
            if p < 2:
                push(w.at[t, 64:80, cols], w.at[t, other_from_x(d), cols], o1_s.at[p], o1_r.at[p], xdev(d))
            else:
                push(w.at[t, 64:80, cols], w.at[t, 64:80, cols], o1_s.at[p], o1_r.at[p], ydev(d))

    nt = (((1,), (1,)), ((), ()))

    def forward(r):
        rows = slice(64 * r, 64 * r + 64)
        gate = lax.dot_general(w[GATE, rows, :], tok[...], nt, preferred_element_type=F32)
        up = lax.dot_general(w[UP, rows, :], tok[...], nt, preferred_element_type=F32)
        back = lax.dot_general(w[DOWN, rows, :], cot[...], nt, preferred_element_type=F32)
        sigma = jax.nn.sigmoid(gate)
        silu = gate * sigma
        act[r, 0] = (silu * up).astype(BF16)
        act[r, 1] = (back * silu).astype(BF16)
        act[r, 2] = (back * up * sigma * (1.0 + gate * (1.0 - sigma))).astype(BF16)

    def terms(r):
        for first, last, src in ((0, 1, cot), (1, 3, tok)):
            n = last - first
            lhs = act[r, first:last].reshape(64 * n, 256)
            for side in range(2):

                @pl.loop(0, 4)
                def _(q):
                    cols = pl.ds(pl.multiple_of((4 * side + q) * 512, 512), 512)
                    t = jnp.dot(lhs, src[:, cols], preferred_element_type=F32).astype(BF16)
                    for j in range(n):
                        k = 3 * r + first + j
                        for a in range(4):
                            for b in range(4):
                                tile = t[64 * j + 16 * a:64 * j + 16 * a + 16, 128 * b:128 * b + 128]
                                if side == 0:
                                    ta[k, a, b, q] = tile
                                else:
                                    tb[k, b, a, q] = tile

            for j in range(n):
                k = 3 * r + first + j
                for d in (2, 1, 3):
                    push(ta.at[k, d], ra.at[k, d - 1], p1_s.at[k, 0], p1_r.at[k, 0], xdev(d))
                    push(tb.at[k, (y + d) % NY], rb.at[k, d - 1], p1_s.at[k, 1], p1_r.at[k, 1], ydev(d))

    drain(tok.at[0:128], core_r.at[0])
    drain(cot.at[0:128], core_r.at[1])
    drain(w.at[GATE, 0:48, 0:3072], own_yr.at[GATE])
    drain(w.at[UP, 0:48, 0:3072], own_yr.at[UP])
    drain(w.at[DOWN, 0:48], own_xr.at[DOWN])
    forward(0)

    for p, (t, cols, n) in enumerate(pieces):
        drain(w.at[t, 0:48, 0:n], o1_r.at[p])
        row = slice(None) if t == DOWN else slice(2048, 4096)
        for d in (2, 1, 3):
            if p < 2:
                push(w.at[t, 64:128, cols], w.at[t, 64:128, cols], o2_s.at[p], o2_r.at[p], ydev(d))
            else:
                push(w.at[t, 64:80, row], w.at[t, other_from_x(d), row], o2_s.at[p], o2_r.at[p], xdev(d))

    terms(0)

    o2_bytes = [w.at[GATE, 0:64, 0:3072], w.at[UP, 0:64, 0:1536], w.at[UP, 0:48, 0:2048], w.at[DOWN, 0:48]]
    for p in range(4):
        drain(o2_bytes[p], o2_r.at[p])
    forward(1)
    terms(1)

    def both(tokens_at):
        parts = [
            jnp.concatenate([act[0, j, :, tokens_at], act[1, j, :, tokens_at]], axis=0).astype(F32).T
            for j in (2, 1)
        ]
        return jnp.concatenate(parts, axis=1).astype(BF16)

    theirs = both(slice(128, 256))

    @pl.loop(0, 8)
    def _(q):
        cols = pl.ds(pl.multiple_of(q * 512, 512), 512)
        rhs = w[GATE:UP + 1, :, cols].reshape(256, 512)
        ig_send[:, cols] = jnp.dot(theirs, rhs, preferred_element_type=F32).astype(BF16)

    push(ig_send, ig_recv, core_s.at[2], core_r.at[2], partner)

    def input_gradient():
        mine = both(slice(0, 128))
        drain(ig_recv, core_r.at[2])

        @pl.loop(0, 8)
        def _(q):
            cols = pl.ds(pl.multiple_of(q * 512, 512), 512)
            rhs = w[GATE:UP + 1, :, cols].reshape(256, 512)
            total = jnp.dot(mine, rhs, preferred_element_type=F32) + ig_recv[:, cols].astype(F32)
            ig_own[:, cols] = total.astype(BF16)

        pltpu.make_async_copy(ig_own, ig_out, load_sem.at[5]).start()

    def plane_sum(own, got):
        return (own + got[0].astype(F32)) + (got[1].astype(F32) + got[2].astype(F32))

    def first(k):
        drain(ra.at[k], p1_r.at[k, 0])
        ua[k] = plane_sum(ta[k, 0].astype(F32), ra[k]).astype(BF16)
        for d in (2, 1, 3):
            push(ua.at[k, (y + d) % NY], va.at[k, d - 1], p2_s.at[k, 0], p2_r.at[k, 0], ydev(d))
        drain(rb.at[k], p1_r.at[k, 1])
        ub[k] = plane_sum(tb[k, y].astype(F32), rb[k]).astype(BF16)
        for d in (2, 1, 3):
            push(ub.at[k, d], vb.at[k, d - 1], p2_s.at[k, 1], p2_r.at[k, 1], xdev(d))

    def second(k):
        r, j = k // 3, k % 3
        drain(va.at[k], p2_r.at[k, 0])
        zs[k, 0:4] = plane_sum(ua[k, y].astype(F32), va[k]).astype(BF16)
        drain(vb.at[k], p2_r.at[k, 1])
        zs[k, 4:8] = plane_sum(ub[k, 0].astype(F32), vb[k]).astype(BF16)
        if r == 0:
            zr[j, z] = zs[k, zl]
        base = (zh if r == 0 else 1 - zh) * ZLO
        for d in range(1 - r, ZLO):
            to = (zl + d) % ZLO
            push(zs.at[k, to], zr.at[j, z], z_s.at[k], z_r.at[j], zdev(base + to))

    first(0)
    first(1)
    input_gradient()
    for k in range(2, 6):
        second(k - 2)
        first(k)
    second(4)
    second(5)
    for j, out in enumerate((dg_out, ug_out, gg_out)):
        drain(zr.at[j, 0:NZ - 1], z_r.at[j])
        out[...] = jnp.sum(zr[j].astype(F32), axis=0) * scale

    pltpu.make_async_copy(ig_own, ig_out, load_sem.at[5]).wait()
    drain(tok.at[0:128], core_s.at[0])
    drain(cot.at[0:128], core_s.at[1])
    drain(ig_send, core_s.at[2])
    for t in (GATE, UP):
        drain(w.at[t, 0:48, 0:1024], own_xs.at[t])
        drain(w.at[t, 0:48, 0:3072], own_ys.at[t])
    drain(w.at[DOWN, 0:48], own_xs.at[DOWN])

    @pl.when(at_edge)
    def _():
        for p, (t, _, n) in enumerate(pieces):
            drain(w.at[t, 0:64, 0:n], hz_s.at[p])

    for p, (t, _, n) in enumerate(pieces):
        drain(w.at[t, 0:48, 0:n], o1_s.at[p])
        drain(o2_bytes[p], o2_s.at[p])
    for k in range(6):
        drain(ra.at[k], p1_s.at[k, 0])
        drain(rb.at[k], p1_s.at[k, 1])
        drain(va.at[k], p2_s.at[k, 0])
        drain(vb.at[k], p2_s.at[k, 1])
        drain(zs.at[k, 0:7 + k // 3], z_s.at[k])


def per_device(tokens, cotangent, gate_weight, up_weight, down_weight):
    token_total = tokens.shape[0] * lax.axis_size("dp") * lax.axis_size("pipe")
    scale = float(token_total) ** (-0.5)
    anywhere = pl.BlockSpec(memory_space=pl.ANY)
    inside = pl.BlockSpec(memory_space=pltpu.VMEM)
    share = jax.ShapeDtypeStruct((16, 128), F32)

    def body(*refs):
        panel_kernel(scale, *refs)

    def held(*shape):
        return pltpu.VMEM(shape, BF16)

    def sems(*shape):
        return pltpu.SemaphoreType.DMA(shape)

    return pl.pallas_call(
        body,
        out_shape=(jax.ShapeDtypeStruct(tokens.shape, BF16), share, share, share),
        in_specs=[anywhere] * 5,
        out_specs=(anywhere, inside, inside, inside),
        scratch_shapes=[
            held(256, 4096), held(256, 4096), held(3, 128, 4096), held(2, 3, 64, 256),
            held(6, 4, 4, 4, 16, 128), held(6, 4, 4, 4, 16, 128),
            held(6, 3, 4, 4, 16, 128), held(6, 3, 4, 4, 16, 128),
            held(6, 4, 4, 16, 128), held(6, 4, 4, 16, 128),
            held(6, 3, 4, 16, 128), held(6, 3, 4, 16, 128),
            held(6, 8, 16, 128), held(3, 16, 16, 128),
            held(128, 4096), held(128, 4096), held(128, 4096),
            sems(6), sems(3), sems(3), sems(3), sems(3), sems(2), sems(2), sems(4), sems(4),
            sems(4), sems(4), sems(4), sems(4),
            sems(6, 2), sems(6, 2), sems(6, 2), sems(6, 2), sems(6), sems(3),
        ],
        compiler_params=pltpu.CompilerParams(
            collective_id=0, has_side_effects=True, vmem_limit_bytes=48 * 2**20
        ),
    )(tokens, cotangent, gate_weight, up_weight, down_weight)


def solution(mesh):
    in_specs = (
        P(("dp", "pipe"), None),
        P(("dp", "pipe"), None),
        P("pipe", None),
        P("pipe", None),
        P("pipe", None),
    )
    out_specs = (P(("dp", "pipe"), None), P("pipe", "dp"), P("pipe", "dp"), P("pipe", "dp"))
    return jax.shard_map(
        per_device, mesh=mesh, in_specs=in_specs, out_specs=out_specs, check_vma=False
    )
```

time: 817 us -> 84.1 us (0.10)
  the two profiles are of different devices: /device:TPU:2 before, /device:TPU:32 now
where the time goes in v1:
time: 84.1 us; the launch traced here: 83.8 us
  Pallas kernels  75.3 us (90%)
  local copies, waits for them, and re-layouts  7.92 us (9%)
    pallas_call x1, Pallas kernels, per_device(): pl.pallas_call(body, out_shape=(jax.ShapeDtypeStruct(tokens.shape, BF16),...  75.3 us
    unnamed x14, local copies, waits for them, and re-layouts  7.92 us

profile of v1, /device:TPU:32, one launch (start us, length us, event | category | flops | bytes accessed | tf_op | source)
XLA Modules:
  0.0 83.8 jit_solution(6260529485200232058)
XLA Ops:
  0.6 0.0 copy-start
  0.6 1.2 %copy-done = bf16[128,4096]{1,0:T(8,128)(2,1)S(1)} copy-done((bf16[128,4096]{1,0:T(8,128)(2,1)S(1)}, bf16[128,4096]{1,0:T(8,128)(2,1)}, u32[]{:S(2)}) %copy-start) | copy-done | bytes 1048600
  1.9 0.0 copy-start.1
  1.9 1.2 %copy-done.1 = bf16[128,4096]{1,0:T(8,128)(2,1)S(1)} copy-done((bf16[128,4096]{1,0:T(8,128)(2,1)S(1)}, bf16[128,4096]{1,0:T(8,128)(2,1)}, u32[]{:S(2)}) %copy-start.1) | copy-done | bytes 1048600
  3.1 0.0 copy-start.2
  3.1 0.9 %copy-done.2 = bf16[16,4096]{1,0:T(8,128)(2,1)S(1)} copy-done((bf16[16,4096]{1,0:T(8,128)(2,1)S(1)}, bf16[16,4096]{1,0:T(8,128)(2,1)}, u32[]{:S(2)}) %copy-start.2) | copy-done | bytes 131096
  4.0 0.0 copy-start.3
  4.0 0.9 %copy-done.3 = bf16[16,4096]{1,0:T(8,128)(2,1)S(1)} copy-done((bf16[16,4096]{1,0:T(8,128)(2,1)S(1)}, bf16[16,4096]{1,0:T(8,128)(2,1)}, u32[]{:S(2)}) %copy-start.3) | copy-done | bytes 131096
  4.9 0.0 copy-start.4
  4.9 0.9 %copy-done.4 = bf16[16,4096]{1,0:T(8,128)(2,1)S(1)} copy-done((bf16[16,4096]{1,0:T(8,128)(2,1)S(1)}, bf16[16,4096]{1,0:T(8,128)(2,1)}, u32[]{:S(2)}) %copy-start.4) | copy-done | bytes 131096
  5.8 75.3 %shard_map.84 = (bf16[128,4096]{1,0:T(8,128)(2,1)S(1)}, f32[16,128]{1,0:T(8,128)S(1)}, f32[16,128]{1,0:T(8,128)S(1)}, f32[16,128]{1,0:T(8,128)S(1)}) custom-call(bf16[128,4096]{1,0:T(8,128)(2,1)S(1)} %copy-done, bf16[128,4096]{1,0:T(8,128)(2,1)S(1)} %copy-done.1, bf16[16,4096]{1,0:T(8,128)(2,1)S(1)} %copy-done.2, bf16[16,4096]{1,0:T(8,128)(2,1)S(1)} %copy-done.3, ...), custom_call_target="tpu_custom_call" | custom-call | tf_op jit(solution)/shard_map/pallas_call | solution.py:290
  81.1 1.0 %copy.13 = bf16[128,4096]{1,0:T(8,128)(2,1)} copy(bf16[128,4096]{1,0:T(8,128)(2,1)S(1)} %get-tuple-element.8) | data formatting | bytes 2097152
  82.0 0.6 copy.14
  82.6 0.6 copy.15
  83.2 0.6 copy.16
Async XLA Ops:
  0.6 1.2 %copy-start = (bf16[128,4096]{1,0:T(8,128)(2,1)S(1)}, bf16[128,4096]{1,0:T(8,128)(2,1)}, u32[]{:S(2)}) copy-start(bf16[128,4096]{1,0:T(8,128)(2,1)} %refs_0_.1) | copy-start | bytes 3145732
  1.9 1.2 %copy-start.1 = (bf16[128,4096]{1,0:T(8,128)(2,1)S(1)}, bf16[128,4096]{1,0:T(8,128)(2,1)}, u32[]{:S(2)}) copy-start(bf16[128,4096]{1,0:T(8,128)(2,1)} %refs_1_.1) | copy-start | bytes 3145732
  3.1 0.9 %copy-start.2 = (bf16[16,4096]{1,0:T(8,128)(2,1)S(1)}, bf16[16,4096]{1,0:T(8,128)(2,1)}, u32[]{:S(2)}) copy-start(bf16[16,4096]{1,0:T(8,128)(2,1)} %refs_2_.1) | copy-start | bytes 393220
  4.0 0.9 %copy-start.3 = (bf16[16,4096]{1,0:T(8,128)(2,1)S(1)}, bf16[16,4096]{1,0:T(8,128)(2,1)}, u32[]{:S(2)}) copy-start(bf16[16,4096]{1,0:T(8,128)(2,1)} %refs_3_.1) | copy-start | bytes 393220
  4.9 0.9 %copy-start.4 = (bf16[16,4096]{1,0:T(8,128)(2,1)S(1)}, bf16[16,4096]{1,0:T(8,128)(2,1)}, u32[]{:S(2)}) copy-start(bf16[16,4096]{1,0:T(8,128)(2,1)} %refs_4_.1) | copy-start | bytes 393220

commit v2 on v1

v2 whole, which is shorter than its diff:
```python
import jax
import jax.numpy as jnp
from jax import lax
from jax.experimental import pallas as pl
from jax.experimental.pallas import tpu as pltpu
from jax.sharding import PartitionSpec as P

F32, BF16 = jnp.float32, jnp.bfloat16
MESH = pl.DeviceIdType.MESH
NX, NY, ZLO, NZ = 4, 4, 8, 16
GATE, UP, DOWN = 0, 1, 2
CHUNKS = ((0, 0, 3), (1, 0, 1), (1, 1, 3))


def panel_kernel(
    scale,
    tok_in, cot_in, wg_in, wu_in, wd_in,
    ig_out, grad_out,
    tok, cot, w, act, ig_send, ig_recv, ig_own,
    load_sem, core_s, core_r, own_xs, own_xr, own_ys, own_yr, hz_s, hz_r, o1_s, o1_r, o2_s, o2_r,
    p1_s, p1_r, p2_s, p2_r, z_s, z_r, reach,
    *bufs,
):
    tas, tbs, ras, rbs, uas, ubs, vas, vbs, zss, zrs = (bufs[3 * i:3 * i + 3] for i in range(10))
    dp, pipe = lax.axis_index("dp"), lax.axis_index("pipe")
    zl, y = dp // NY, dp % NY
    zh, x, c = pipe // 8, (pipe // 2) % NX, pipe % 2
    z = zh * ZLO + zl

    def dev(x_, y_, z_, c_):
        return ((z_ % ZLO) * NY + y_, ((z_ // ZLO) * NX + x_) * 2 + c_)

    def xdev(d):
        return dev((x + d) % NX, y, z, c)

    def ydev(d):
        return dev(x, (y + d) % NY, z, c)

    def zdev(z_):
        return dev(x, y, z_ % NZ, c)

    partner = dev(x, y, z, 1 - c)

    def push(src, dst, ssem, rsem, to):
        pltpu.make_async_remote_copy(src, dst, ssem, rsem, device_id=to, device_id_type=MESH).start()

    def drain(ref, sem):
        pltpu.make_async_copy(ref, ref, sem).wait()

    loads = [
        pltpu.make_async_copy(src, dst, load_sem.at[i])
        for i, (src, dst) in enumerate([
            (wg_in, w.at[GATE, 0:16]), (wu_in, w.at[UP, 0:16]), (wd_in, w.at[DOWN, 0:16]),
            (tok_in, tok.at[0:128]), (cot_in, cot.at[0:128]),
        ])
    ]
    for cp in loads:
        cp.start()

    barrier = pltpu.get_barrier_semaphore()

    def greet(to):
        pl.semaphore_signal(barrier, inc=1, device_id=to, device_id_type=MESH)

    greet(partner)
    for d in range(1, 4):
        greet(xdev(d))
        greet(ydev(d))

    for d in range(1, 5):
        greet(zdev(z + d))
        greet(zdev(z + NZ - d))
    pl.semaphore_wait(barrier, 15)
    for d in (4, NZ - 4):
        pl.semaphore_signal(reach, inc=1, device_id=zdev(z + d), device_id_type=MESH)

    quarter = pl.ds(pl.multiple_of(y * 1024, 1024), 1024)
    eighth0 = pl.ds(pl.multiple_of(y * 512, 512), 512)
    eighth1 = pl.ds(pl.multiple_of(2048 + y * 512, 512), 512)
    pieces = [
        (DOWN, quarter, 1024, False), (UP, eighth1, 512, False), (GATE, quarter, 1024, True), (UP, eighth0, 512, True),
    ]

    def from_x(d):
        return pl.ds(16 * (4 - d), 16)

    def other_from_x(d):
        return pl.ds(64 + 16 * (4 - d), 16)

    for cp in loads[:3]:
        cp.wait()
    for t in (GATE, UP):
        for d in (2, 1, 3):
            push(w.at[t, 0:16, quarter], w.at[t, from_x(d), quarter], own_xs.at[t], own_xr.at[t], xdev(d))
    at_edge = (zl == 0) | (zl == ZLO - 1)
    step = jnp.where(zl == 0, NZ - 1, 1)

    @pl.when(at_edge)
    def _():
        for p, (t, cols, _, _) in enumerate(pieces):
            for dist in (4, 3, 2, 1):
                push(w.at[t, 0:16, cols], w.at[t, 64:80, cols], hz_s.at[p], hz_r.at[p], zdev(z + step * dist))

    loads[3].wait()
    push(tok.at[0:128], tok.at[128:256], core_s.at[0], core_r.at[0], partner)
    loads[4].wait()
    push(cot.at[0:128], cot.at[128:256], core_s.at[1], core_r.at[1], partner)
    for d in (2, 1, 3):
        push(w.at[DOWN, 0:16], w.at[DOWN, from_x(d)], own_xs.at[DOWN], own_xr.at[DOWN], xdev(d))

    def own_by_y(t):
        drain(w.at[t, 0:48, 0:1024], own_xr.at[t])
        for d in (2, 1, 3):
            push(w.at[t, 16:64, quarter], w.at[t, 16:64, quarter], own_ys.at[t], own_yr.at[t], ydev(d))

    def other_one(p):
        t, cols, n, by_x = pieces[p]
        drain(w.at[t, 0:16, 0:n], hz_r.at[p])
        for d in (2, 1, 3):
            if by_x:
                push(w.at[t, 64:80, cols], w.at[t, other_from_x(d), cols], o1_s.at[p], o1_r.at[p], xdev(d))
            else:
                push(w.at[t, 64:80, cols], w.at[t, 64:80, cols], o1_s.at[p], o1_r.at[p], ydev(d))

    def other_two(p):
        t, cols, n, by_x = pieces[p]
        drain(w.at[t, 0:48, 0:n], o1_r.at[p])
        row = slice(None) if t == DOWN else slice(2048, 4096)
        for d in (2, 1, 3):
            if by_x:
                push(w.at[t, 64:128, cols], w.at[t, 64:128, cols], o2_s.at[p], o2_r.at[p], ydev(d))
            else:
                push(w.at[t, 64:80, row], w.at[t, other_from_x(d), row], o2_s.at[p], o2_r.at[p], xdev(d))

    own_by_y(GATE)
    other_one(0)
    other_one(1)
    own_by_y(UP)
    other_one(2)
    other_one(3)
    for p in range(4):
        other_two(p)

    nt = (((1,), (1,)), ((), ()))

    def forward(r):
        rows = slice(64 * r, 64 * r + 64)
        gate = lax.dot_general(w[GATE, rows, :], tok[...], nt, preferred_element_type=F32)
        up = lax.dot_general(w[UP, rows, :], tok[...], nt, preferred_element_type=F32)
        back = lax.dot_general(w[DOWN, rows, :], cot[...], nt, preferred_element_type=F32)
        sigma = jax.nn.sigmoid(gate)
        silu = gate * sigma
        act[r, 0] = (silu * up).astype(BF16)
        act[r, 1] = (back * silu).astype(BF16)
        act[r, 2] = (back * up * sigma * (1.0 + gate * (1.0 - sigma))).astype(BF16)

    def terms(k):
        r, start, end = CHUNKS[k]
        for first, last, src in ((0, 1, cot), (1, 3, tok)):
            if not start <= first < end:
                continue
            n = last - first
            lhs = act[r, first:last].reshape(64 * n, 256)
            for side in range(2):

                @pl.loop(0, 4)
                def _(q):
                    cols = pl.ds(pl.multiple_of((4 * side + q) * 512, 512), 512)
                    t = jnp.dot(lhs, src[:, cols], preferred_element_type=F32).astype(BF16)
                    for j in range(n):
                        at = first - start + j
                        for a in range(4):
                            for b in range(4):
                                tile = t[64 * j + 16 * a:64 * j + 16 * a + 16, 128 * b:128 * b + 128]
                                if side == 0:
                                    tas[k][a, b, at, q] = tile
                                else:
                                    tbs[k][b, a, at, q] = tile

                if last == end:
                    for d in (2, 1, 3):
                        if side == 0:
                            push(tas[k].at[d], ras[k].at[d - 1], p1_s.at[k, 0], p1_r.at[k, 0], xdev(d))
                        else:
                            push(tbs[k].at[(y + d) % NY], rbs[k].at[d - 1], p1_s.at[k, 1], p1_r.at[k, 1], ydev(d))

    drain(tok.at[0:128], core_r.at[0])
    drain(cot.at[0:128], core_r.at[1])
    drain(w.at[GATE, 0:48, 0:3072], own_yr.at[GATE])
    drain(w.at[UP, 0:48, 0:3072], own_yr.at[UP])
    drain(w.at[DOWN, 0:48], own_xr.at[DOWN])
    forward(0)
    terms(0)

    o2_bytes = [w.at[DOWN, 0:48], w.at[UP, 0:48, 0:2048], w.at[GATE, 0:64, 0:3072], w.at[UP, 0:64, 0:1536]]
    for p in range(4):
        drain(o2_bytes[p], o2_r.at[p])
    forward(1)
    terms(1)
    terms(2)

    def both(tokens_at):
        parts = [
            jnp.concatenate([act[0, j, :, tokens_at], act[1, j, :, tokens_at]], axis=0).astype(F32).T
            for j in (2, 1)
        ]
        return jnp.concatenate(parts, axis=1).astype(BF16)

    theirs = both(slice(128, 256))

    @pl.loop(0, 8)
    def _(q):
        cols = pl.ds(pl.multiple_of(q * 512, 512), 512)
        rhs = w[GATE:UP + 1, :, cols].reshape(256, 512)
        ig_send[:, cols] = jnp.dot(theirs, rhs, preferred_element_type=F32).astype(BF16)

    push(ig_send, ig_recv, core_s.at[2], core_r.at[2], partner)

    def input_gradient():
        mine = both(slice(0, 128))
        drain(ig_recv, core_r.at[2])

        @pl.loop(0, 8)
        def _(q):
            cols = pl.ds(pl.multiple_of(q * 512, 512), 512)
            rhs = w[GATE:UP + 1, :, cols].reshape(256, 512)
            total = jnp.dot(mine, rhs, preferred_element_type=F32) + ig_recv[:, cols].astype(F32)
            ig_own[:, cols] = total.astype(BF16)

        pltpu.make_async_copy(ig_own, ig_out, load_sem.at[5]).start()

    def plane_sum(own, got):
        return ((own.astype(F32) + got[0].astype(F32)) + (got[1].astype(F32) + got[2].astype(F32))).astype(BF16)

    def first(k):
        ta, tb, ra, rb, ua, ub, va, vb = (b[k] for b in (tas, tbs, ras, rbs, uas, ubs, vas, vbs))
        drain(ra, p1_r.at[k, 0])
        for d in (2, 1, 3, 0):
            to = (y + d) % NY
            ua[to] = plane_sum(ta[0, to], ra[:, to])
            if d:
                push(ua.at[to], va.at[d - 1], p2_s.at[k, 0], p2_r.at[k, 0], ydev(d))
        drain(rb, p1_r.at[k, 1])
        for d in (2, 1, 3, 0):
            ub[d] = plane_sum(tb[y, d], rb[:, d])
            if d:
                push(ub.at[d], vb.at[d - 1], p2_s.at[k, 1], p2_r.at[k, 1], xdev(d))

    def second(k):
        r = CHUNKS[k][0]
        ua, ub, va, vb, zs, zr = (b[k] for b in (uas, ubs, vas, vbs, zss, zrs))
        n = zs.shape[1]
        drain(va, p2_r.at[k, 0])
        for j in range(n):
            zs[0:4, j] = plane_sum(ua[y, j], va[:, j])
        drain(vb, p2_r.at[k, 1])
        for j in range(n):
            zs[4:8, j] = plane_sum(ub[0, j], vb[:, j])
        if r == 0:
            zr[zl] = zs[zl]
        base = (zh if r == 0 else 1 - zh) * ZLO
        for d in ((4, 3, 5, 2, 6, 1, 7) if r == 0 else range(ZLO)):
            to = (zl + d) % ZLO
            push(zs.at[to], zr.at[zl], z_s.at[k], z_r.at[k], zdev(base + to))

    pl.semaphore_wait(reach, 2)
    first(0)
    input_gradient()
    second(0)
    first(1)
    first(2)
    second(1)
    second(2)
    for k, (r, _, _) in enumerate(CHUNKS):
        drain(zrs[k].at[0:7 + r], z_r.at[k])
    for j in range(3):
        late = zrs[1][:, 0] if j == 0 else zrs[2][:, j - 1]
        grad_out[j] = (jnp.sum(zrs[0][:, j].astype(F32), axis=0) + jnp.sum(late.astype(F32), axis=0)) * scale

    pltpu.make_async_copy(ig_own, ig_out, load_sem.at[5]).wait()
    drain(tok.at[0:128], core_s.at[0])
    drain(cot.at[0:128], core_s.at[1])
    drain(ig_send, core_s.at[2])
    for t in (GATE, UP):
        drain(w.at[t, 0:48, 0:1024], own_xs.at[t])
        drain(w.at[t, 0:48, 0:3072], own_ys.at[t])
    drain(w.at[DOWN, 0:48], own_xs.at[DOWN])

    @pl.when(at_edge)
    def _():
        for p, (t, _, n, _) in enumerate(pieces):
            drain(w.at[t, 0:64, 0:n], hz_s.at[p])

    for p, (t, _, n, _) in enumerate(pieces):
        drain(w.at[t, 0:48, 0:n], o1_s.at[p])
        drain(o2_bytes[p], o2_s.at[p])
    for k, (r, _, _) in enumerate(CHUNKS):
        drain(ras[k], p1_s.at[k, 0])
        drain(rbs[k], p1_s.at[k, 1])
        drain(vas[k], p2_s.at[k, 0])
        drain(vbs[k], p2_s.at[k, 1])
        drain(zss[k].at[0:7 + r], z_s.at[k])


def finish_kernel(ig, grads, ig_out, gate_out, up_out, down_out, sem):
    pairs = [(ig.at[pl.ds(32 * i, 32)], ig_out.at[pl.ds(32 * i, 32)]) for i in range(4)]
    pairs += [(grads.at[2], gate_out), (grads.at[1], up_out), (grads.at[0], down_out)]
    copies = [pltpu.make_async_copy(src, dst, sem.at[i]) for i, (src, dst) in enumerate(pairs)]
    for cp in copies:
        cp.start()
    for cp in copies:
        cp.wait()


def per_device(tokens, cotangent, gate_weight, up_weight, down_weight):
    token_total = tokens.shape[0] * lax.axis_size("dp") * lax.axis_size("pipe")
    scale = float(token_total) ** (-0.5)
    anywhere = pl.BlockSpec(memory_space=pl.ANY)
    inside = pl.BlockSpec(memory_space=pltpu.VMEM)
    share = jax.ShapeDtypeStruct((16, 128), F32)

    def body(*refs):
        panel_kernel(scale, *refs)

    def held(*shape):
        return pltpu.VMEM(shape, BF16)

    def sems(*shape):
        return pltpu.SemaphoreType.DMA(shape)

    def chunked(*dims):
        shapes = [[last - first if d is None else d for d in dims] for _, first, last in CHUNKS]
        return [held(*dims_, 16, 128) for dims_ in shapes]

    ig, grads = pl.pallas_call(
        body,
        out_shape=(jax.ShapeDtypeStruct(tokens.shape, BF16), jax.ShapeDtypeStruct((3, 16, 128), F32)),
        in_specs=[anywhere] * 5,
        out_specs=(anywhere, inside),
        scratch_shapes=[
            held(256, 4096), held(256, 4096), held(3, 128, 4096), held(2, 3, 64, 256),
            held(128, 4096), held(128, 4096), held(128, 4096),
            sems(6), sems(3), sems(3), sems(3), sems(3), sems(2), sems(2), sems(4), sems(4),
            sems(4), sems(4), sems(4), sems(4),
            sems(3, 2), sems(3, 2), sems(3, 2), sems(3, 2), sems(3), sems(3), pltpu.SemaphoreType.REGULAR,
            *chunked(4, 4, None, 4), *chunked(4, 4, None, 4), *chunked(3, 4, None, 4), *chunked(3, 4, None, 4),
            *chunked(4, None, 4), *chunked(4, None, 4), *chunked(3, None, 4), *chunked(3, None, 4),
            *chunked(8, None), *chunked(8, None),
        ],
        compiler_params=pltpu.CompilerParams(
            collective_id=0, has_side_effects=True, vmem_limit_bytes=60 * 2**20
        ),
    )(tokens, cotangent, gate_weight, up_weight, down_weight)
    return pl.pallas_call(
        finish_kernel,
        out_shape=(jax.ShapeDtypeStruct(tokens.shape, BF16), share, share, share),
        in_specs=[inside] * 2,
        out_specs=[anywhere] * 4,
        scratch_shapes=[sems(7)],
    )(ig, grads)


def solution(mesh):
    in_specs = (
        P(("dp", "pipe"), None),
        P(("dp", "pipe"), None),
        P("pipe", None),
        P("pipe", None),
        P("pipe", None),
    )
    out_specs = (P(("dp", "pipe"), None), P("pipe", "dp"), P("pipe", "dp"), P("pipe", "dp"))
    return jax.shard_map(
        per_device, mesh=mesh, in_specs=in_specs, out_specs=out_specs, check_vma=False
    )
```

time: 84.1 us -> 75.1 us (0.89)
  the two profiles are of different devices: /device:TPU:32 before, /device:TPU:64 now
where the time goes in v2:
time: 75.1 us; the launch traced here: 74.9 us
  Pallas kernels  74.3 us (99%)
    pallas_call x1, Pallas kernels, per_device(): pl.pallas_call(body, out_shape=(jax.ShapeDtypeStruct(tokens.shape, BF16),...  72 us
    pallas_call x1, Pallas kernels, per_device(): pl.pallas_call(finish_kernel, out_shape=(jax.ShapeDtypeStruct(tokens.shap...  2.25 us

profile of v2, /device:TPU:64, one launch (start us, length us, event | category | flops | bytes accessed | tf_op | source)
XLA Modules:
  0.0 74.9 jit_solution(2575398704560024064)
XLA Ops:
  0.6 72.0 %shard_map.84 = (bf16[128,4096]{1,0:T(8,128)(2,1)}, f32[3,16,128]{2,1,0:T(8,128)}) custom-call(bf16[128,4096]{1,0:T(8,128)(2,1)} %refs_0_.1, bf16[128,4096]{1,0:T(8,128)(2,1)} %refs_1_.1, bf16[16,4096]{1,0:T(8,128)(2,1)} %refs_2_.1, bf16[16,4096]{1,0:T(8,128)(2,1)} %refs_3_.1, bf16[16,4096]{1,0:T(8,128)(2,1)} %refs_4_.1), custom_call_target="tpu_custom_call" | custom-call | tf_op jit(solution)/shard_map/pallas_call | solution.py:335
  72.7 2.3 %shard_map.85 = (bf16[128,4096]{1,0:T(8,128)(2,1)}, f32[16,128]{1,0:T(8,128)}, f32[16,128]{1,0:T(8,128)}, f32[16,128]{1,0:T(8,128)}) custom-call(bf16[128,4096]{1,0:T(8,128)(2,1)} %get-tuple-element.6.ig, f32[3,16,128]{2,1,0:T(8,128)} %get-tuple-element.7.grads), custom_call_target="tpu_custom_call" | custom-call | tf_op jit(solution)/shard_map/pallas_call | solution.py:354

commit v3 on v2

--- a/solution.py
+++ b/solution.py
@@ -101,10 +101,6 @@
             for dist in (4, 3, 2, 1):
                 push(w.at[t, 0:16, cols], w.at[t, 64:80, cols], hz_s.at[p], hz_r.at[p], zdev(z + step * dist))
 
-    loads[3].wait()
-    push(tok.at[0:128], tok.at[128:256], core_s.at[0], core_r.at[0], partner)
-    loads[4].wait()
-    push(cot.at[0:128], cot.at[128:256], core_s.at[1], core_r.at[1], partner)
     for d in (2, 1, 3):
         push(w.at[DOWN, 0:16], w.at[DOWN, from_x(d)], own_xs.at[DOWN], own_xr.at[DOWN], xdev(d))
 
@@ -133,6 +129,10 @@
                 push(w.at[t, 64:80, row], w.at[t, other_from_x(d), row], o2_s.at[p], o2_r.at[p], xdev(d))
 
     own_by_y(GATE)
+    loads[3].wait()
+    push(tok.at[0:128], tok.at[128:256], core_s.at[0], core_r.at[0], partner)
+    loads[4].wait()
+    push(cot.at[0:128], cot.at[128:256], core_s.at[1], core_r.at[1], partner)
     other_one(0)
     other_one(1)
     own_by_y(UP)
@@ -265,10 +265,10 @@
 
     pl.semaphore_wait(reach, 2)
     first(0)
+    first(1)
     input_gradient()
+    first(2)
     second(0)
-    first(1)
-    first(2)
     second(1)
     second(2)
     for k, (r, _, _) in enumerate(CHUNKS):

time: 75.1 us -> 72.4 us (0.964)
  the two profiles are of different devices: /device:TPU:64 before, /device:TPU:8 now
where the time goes in v3:
time: 72.4 us; the launch traced here: 72.3 us
  Pallas kernels  71.7 us (99%)
    pallas_call x1, Pallas kernels, per_device(): pl.pallas_call(body, out_shape=(jax.ShapeDtypeStruct(tokens.shape, BF16),...  69.4 us
    pallas_call x1, Pallas kernels, per_device(): pl.pallas_call(finish_kernel, out_shape=(jax.ShapeDtypeStruct(tokens.shap...  2.25 us

profile of v3, /device:TPU:8, one launch (start us, length us, event | category | flops | bytes accessed | tf_op | source)
XLA Modules:
  0.0 72.3 jit_solution(6143884655926935852)
XLA Ops:
  0.6 69.4 %shard_map.84 = (bf16[128,4096]{1,0:T(8,128)(2,1)}, f32[3,16,128]{2,1,0:T(8,128)}) custom-call(bf16[128,4096]{1,0:T(8,128)(2,1)} %refs_0_.1, bf16[128,4096]{1,0:T(8,128)(2,1)} %refs_1_.1, bf16[16,4096]{1,0:T(8,128)(2,1)} %refs_2_.1, bf16[16,4096]{1,0:T(8,128)(2,1)} %refs_3_.1, bf16[16,4096]{1,0:T(8,128)(2,1)} %refs_4_.1), custom_call_target="tpu_custom_call" | custom-call | tf_op jit(solution)/shard_map/pallas_call | solution.py:335
  70.0 2.3 %shard_map.85 = (bf16[128,4096]{1,0:T(8,128)(2,1)}, f32[16,128]{1,0:T(8,128)}, f32[16,128]{1,0:T(8,128)}, f32[16,128]{1,0:T(8,128)}) custom-call(bf16[128,4096]{1,0:T(8,128)(2,1)} %get-tuple-element.6.ig, f32[3,16,128]{2,1,0:T(8,128)} %get-tuple-element.7.grads), custom_call_target="tpu_custom_call" | custom-call | tf_op jit(solution)/shard_map/pallas_call | solution.py:354

commit v4 on v3

--- a/solution.py
+++ b/solution.py
@@ -143,11 +143,16 @@
 
     nt = (((1,), (1,)), ((), ()))
 
-    def forward(r):
+    def forward(r, arrive):
         rows = slice(64 * r, 64 * r + 64)
+        arrive(0)
+        back = lax.dot_general(w[DOWN, rows, :], cot[...], nt, preferred_element_type=F32)
+        arrive(1)
+        up = lax.dot_general(w[UP, rows, 2048:4096], tok[:, 2048:4096], nt, preferred_element_type=F32)
+        arrive(2)
         gate = lax.dot_general(w[GATE, rows, :], tok[...], nt, preferred_element_type=F32)
-        up = lax.dot_general(w[UP, rows, :], tok[...], nt, preferred_element_type=F32)
-        back = lax.dot_general(w[DOWN, rows, :], cot[...], nt, preferred_element_type=F32)
+        arrive(3)
+        up = up + lax.dot_general(w[UP, rows, 0:2048], tok[:, 0:2048], nt, preferred_element_type=F32)
         sigma = jax.nn.sigmoid(gate)
         silu = gate * sigma
         act[r, 0] = (silu * up).astype(BF16)
@@ -189,13 +194,11 @@
     drain(w.at[GATE, 0:48, 0:3072], own_yr.at[GATE])
     drain(w.at[UP, 0:48, 0:3072], own_yr.at[UP])
     drain(w.at[DOWN, 0:48], own_xr.at[DOWN])
-    forward(0)
+    forward(0, lambda p: None)
     terms(0)
 
     o2_bytes = [w.at[DOWN, 0:48], w.at[UP, 0:48, 0:2048], w.at[GATE, 0:64, 0:3072], w.at[UP, 0:64, 0:1536]]
-    for p in range(4):
-        drain(o2_bytes[p], o2_r.at[p])
-    forward(1)
+    forward(1, lambda p: drain(o2_bytes[p], o2_r.at[p]))
     terms(1)
     terms(2)
 

time: 72.4 us -> 72.3 us (level)
  no operation moved by 1% of the time
where the time goes in v4:
time: 72.3 us; the launch traced here: 72.1 us
  Pallas kernels  71.5 us (99%)
    pallas_call x1, Pallas kernels, per_device(): pl.pallas_call(body, out_shape=(jax.ShapeDtypeStruct(tokens.shape, BF16),...  69.2 us
    pallas_call x1, Pallas kernels, per_device(): pl.pallas_call(finish_kernel, out_shape=(jax.ShapeDtypeStruct(tokens.shap...  2.25 us

profile of v4, /device:TPU:8, one launch (start us, length us, event | category | flops | bytes accessed | tf_op | source)
XLA Modules:
  0.0 72.1 jit_solution(14642839090831564079)
XLA Ops:
  0.6 69.2 %shard_map.84 = (bf16[128,4096]{1,0:T(8,128)(2,1)}, f32[3,16,128]{2,1,0:T(8,128)}) custom-call(bf16[128,4096]{1,0:T(8,128)(2,1)} %refs_0_.1, bf16[128,4096]{1,0:T(8,128)(2,1)} %refs_1_.1, bf16[16,4096]{1,0:T(8,128)(2,1)} %refs_2_.1, bf16[16,4096]{1,0:T(8,128)(2,1)} %refs_3_.1, bf16[16,4096]{1,0:T(8,128)(2,1)} %refs_4_.1), custom_call_target="tpu_custom_call" | custom-call | tf_op jit(solution)/shard_map/pallas_call | solution.py:338
  69.9 2.3 %shard_map.85 = (bf16[128,4096]{1,0:T(8,128)(2,1)}, f32[16,128]{1,0:T(8,128)}, f32[16,128]{1,0:T(8,128)}, f32[16,128]{1,0:T(8,128)}) custom-call(bf16[128,4096]{1,0:T(8,128)(2,1)} %get-tuple-element.6.ig, f32[3,16,128]{2,1,0:T(8,128)} %get-tuple-element.7.grads), custom_call_target="tpu_custom_call" | custom-call | tf_op jit(solution)/shard_map/pallas_call | solution.py:357
